TPU v7x, 512 devices: a whole 4x4x16 slice. The times are simulated.
512 devices in a mesh: row: 32 (over y, z_lo, core), col: 16 (over x, z_hi).
Axes of the slice: x: 4, y: 4, z: 16 (z_hi: 4, z_lo: 4; z = z_hi * 4 + z_lo), core: 2. Of those that a mesh axis runs over, the one named last changes fastest.
Arguments:
- queries: bfloat16 [128, 1024, 1024], P('row', 'col'), may hold values from -5 to 5
- key_vectors: bfloat16 [128, 1024, 1024], P('row', 'col'), may hold values from -5 to 5
- values: bfloat16 [128, 1024, 1024], P('row', 'col'), may hold values from -6 to 6
- out_weight: bfloat16 [1024, 1024], replicated, may hold values from -0.1875 to 0.1875
Outputs:
- attended: bfloat16 [128, 1024, 1024], P('row', 'col')
All inputs are finite; a program needn't handle non-finite values.
Results may differ from a plain program's by a relative error of at most 0.0095.
Values may be sent and summed in bfloat16 or wider, within the bound.
A program may use at most 64 MiB of HBM per device.

v0:
```python
import jax
import jax.numpy as jnp
from jax import lax
from jax.sharding import PartitionSpec as P

HEADS = 8
HEAD_DIM = 128


masked_fill = -1e30


def for_sending(array):

    def short(part):
        return part.astype(jnp.bfloat16) if part.dtype == jnp.float32 else part

    return jax.tree.map(short, array)


def to_items(tensor, rows_dev, cols_dev):
    return (
        tensor.reshape(rows_dev, cols_dev, HEADS, -1)
        .transpose(2, 0, 1, 3)
        .reshape(HEADS * rows_dev, cols_dev, -1)
    )


def from_items(tensor, rows_dev, cols_dev):
    return tensor.reshape(HEADS, rows_dev, cols_dev, -1).transpose(1, 2, 0, 3)


def reduce_set(summed, best, totals):
    floor_total = jnp.maximum(totals, 1.0)
    part = (summed / floor_total[..., None]).astype(jnp.bfloat16)
    level = (best + jnp.log(floor_total)).astype(jnp.bfloat16)
    return (part, level)


def one_item(item):
    query_rows, key_rows, value_rows = item
    width = query_rows.shape[0]
    tri_mask = lax.broadcasted_iota(jnp.int32, (width, width), 0) >= lax.broadcasted_iota(
        jnp.int32, (width, width), 1
    )
    scores = jnp.einsum(
        "jd,kd->jk", query_rows, key_rows, preferred_element_type=jnp.float32
    ) * HEAD_DIM ** (-0.5)
    best = jnp.max(jnp.where(tri_mask, scores, masked_fill), axis=-1)
    weights = jnp.where(tri_mask, jnp.exp(scores - best[:, None]), 0.0)
    totals = jnp.sum(weights, axis=-1)
    summed = jnp.dot(weights.astype(jnp.bfloat16), value_rows, preferred_element_type=jnp.float32)
    return reduce_set(summed, best, totals)


def row_attention(queries, key_vectors, values):
    rows_dev, cols_dev, width = queries.shape
    sent = (
        to_items(queries, rows_dev, cols_dev),
        to_items(key_vectors, rows_dev, cols_dev),
        to_items(values, rows_dev, cols_dev),
    )
    query_items, key_items, value_items = (
        lax.all_to_all(sent[0], "col", split_axis=0, concat_axis=1, tiled=True),
        lax.all_to_all(sent[1], "col", split_axis=0, concat_axis=1, tiled=True),
        lax.all_to_all(sent[2], "col", split_axis=0, concat_axis=1, tiled=True),
    )
    return lax.map(one_item, (query_items, key_items, value_items))


def column_attention(queries, key_vectors, values):
    rows_dev, cols_dev, width = queries.shape
    query_cols, key_cols, value_cols = (
        lax.all_to_all(queries, "row", split_axis=1, concat_axis=0, tiled=True),
        lax.all_to_all(key_vectors, "row", split_axis=1, concat_axis=0, tiled=True),
        lax.all_to_all(values, "row", split_axis=1, concat_axis=0, tiled=True),
    )
    depth, narrow, width = query_cols.shape
    shape_four = (depth, narrow, HEADS, HEAD_DIM)
    lower_mask = lax.broadcasted_iota(jnp.int32, (depth, depth), 0) > lax.broadcasted_iota(
        jnp.int32, (depth, depth), 1
    )
    scores = jnp.einsum(
        "rchd,schd->chrs",
        query_cols.reshape(shape_four),
        key_cols.reshape(shape_four),
        preferred_element_type=jnp.float32,
    ) * HEAD_DIM ** (-0.5)
    best = jnp.max(jnp.where(lower_mask, scores, masked_fill), axis=-1)
    weights = jnp.where(lower_mask, jnp.exp(scores - best[..., None]), 0.0)
    totals = jnp.sum(weights, axis=-1)
    summed = jnp.einsum(
        "chrs,schd->rchd",
        weights.astype(jnp.bfloat16),
        value_cols.reshape(shape_four),
        preferred_element_type=jnp.float32,
    )
    part, level = reduce_set(summed, best.transpose(2, 0, 1), totals.transpose(2, 0, 1))
    parts = (part.reshape(depth, narrow, width), level)
    return (
        lax.all_to_all(parts[0], "row", split_axis=0, concat_axis=1, tiled=True),
        lax.all_to_all(parts[1], "row", split_axis=0, concat_axis=1, tiled=True),
    )


def combine(first_part, first_level, second_part, second_level):
    first_level = first_level.astype(jnp.float32)
    second_level = second_level.astype(jnp.float32)
    top = jnp.maximum(first_level, second_level)
    first_factor = jnp.exp(first_level - top)
    second_factor = jnp.exp(second_level - top)
    numer = first_factor[..., None] * first_part.astype(jnp.float32) + second_factor[
        ..., None
    ] * second_part.astype(jnp.float32)
    denom = first_factor + second_factor
    return (numer / denom[..., None]).astype(jnp.bfloat16)


def body(queries, key_vectors, values, out_weight):
    rows_dev, cols_dev, width = queries.shape
    row_parts = row_attention(queries, key_vectors, values)
    col_part, col_level = column_attention(queries, key_vectors, values)
    row_part, row_level = jax.tree.map(
        lambda part, own: part.astype(own.dtype),
        lax.all_to_all(for_sending(row_parts), "col", split_axis=1, concat_axis=0, tiled=True),
        row_parts,
    )
    row_part = from_items(row_part, rows_dev, cols_dev)
    row_level = from_items(row_level[..., None], rows_dev, cols_dev)[..., 0]
    context = combine(
        row_part, row_level, col_part.reshape(rows_dev, cols_dev, HEADS, HEAD_DIM), col_level
    )
    flat = context.reshape(rows_dev * cols_dev, width)
    attended = jnp.dot(flat, out_weight, preferred_element_type=jnp.float32).astype(jnp.bfloat16)
    return attended.reshape(rows_dev, cols_dev, width)


def solution(mesh):
    in_specs = (P("row", "col", None), P("row", "col", None), P("row", "col", None), P())
    out_specs = P("row", "col", None)
    return jax.shard_map(body, mesh=mesh, in_specs=in_specs, out_specs=out_specs, check_vma=False)
```

profile of v0, /device:TPU:1, one launch (start us, length us, event | category | flops | bytes accessed | tf_op | source)
XLA Modules:
  0.0 298.7 jit_solution(18028188073847879645)
XLA Ops:
  2.3 18.3 %all-to-all-start.1 = ((bf16[32,64,128]{2,1,0:T(8,128)(2,1)}), bf16[32,64,128]{2,1,0:T(8,128)(2,1)}, u32[]{:S(2)}, u32[]{:S(2)}) async-start(bf16[32,64,128]{2,1,0:T(8,128)(2,1)} %bitcast.145), calls=%async_computation.1 | async-start | bytes 1048576 | tf_op jit(solution)/shard_map/all_to_all | solution.py:65
  21.6 26.1 %all-to-all-done.1 = bf16[32,64,128]{2,1,0:T(8,128)(2,1)} async-done(((bf16[32,64,128]{2,1,0:T(8,128)(2,1)}), bf16[32,64,128]{2,1,0:T(8,128)(2,1)}, u32[]{:S(2)}, u32[]{:S(2)}) %all-to-all-start.1) | async-done | bytes 524320 | tf_op jit(solution)/shard_map/all_to_all | solution.py:65
  47.7 8.6 %all-to-all-start.2 = ((bf16[32,64,128]{2,1,0:T(8,128)(2,1)}), bf16[32,64,128]{2,1,0:T(8,128)(2,1)S(1)}, u32[]{:S(2)}, u32[]{:S(2)}) async-start(bf16[32,64,128]{2,1,0:T(8,128)(2,1)} %bitcast.144), calls=%async_computation.2 | async-start | bytes 1048576 | tf_op jit(solution)/shard_map/all_to_all | solution.py:66
  57.3 19.4 %all-to-all-done.2 = bf16[32,64,128]{2,1,0:T(8,128)(2,1)S(1)} async-done(((bf16[32,64,128]{2,1,0:T(8,128)(2,1)}), bf16[32,64,128]{2,1,0:T(8,128)(2,1)S(1)}, u32[]{:S(2)}, u32[]{:S(2)}) %all-to-all-start.2) | async-done | bytes 524320 | tf_op jit(solution)/shard_map/all_to_all | solution.py:66
  76.7 4.2 %all-to-all-start = ((bf16[32,64,128]{2,1,0:T(8,128)(2,1)}), bf16[32,64,128]{2,1,0:T(8,128)(2,1)}, u32[]{:S(2)}, u32[]{:S(2)}) async-start(bf16[32,64,128]{2,1,0:T(8,128)(2,1)} %bitcast.143), calls=%async_computation | async-start | bytes 1048576 | tf_op jit(solution)/shard_map/all_to_all | solution.py:64
  83.7 14.8 %all-to-all-done = bf16[32,64,128]{2,1,0:T(8,128)(2,1)} async-done(((bf16[32,64,128]{2,1,0:T(8,128)(2,1)}), bf16[32,64,128]{2,1,0:T(8,128)(2,1)}, u32[]{:S(2)}, u32[]{:S(2)}) %all-to-all-start) | async-done | bytes 524320 | tf_op jit(solution)/shard_map/all_to_all | solution.py:64
  100.4 8.1 %while.12 = (s32[]{:T(128)}, bf16[2,1024,128]{2,1,0:T(8,128)(2,1)}, bf16[2,1024]{1,0:T(2,128)(2,1)S(1)}, bf16[2,1024,128]{2,1,0:T(8,128)(2,1)}, bf16[2,1024,128]...) while((s32[]{:T(128)}, bf16[2,1024,128]{2,1,0:T(8,128)(2,1)}, ...), condition=%wide.region_3.4_spmd, body=%wide.region_0.3_spmd.sunk | while | flops 551814144 | bytes 19968172 | solution.py:68
  109.2 3.5 %all-to-all-start.3 = ((bf16[2,16,64]{2,0,1:T(2,128)(2,1)}), bf16[2,16,64]{2,0,1:T(2,128)(2,1)S(1)}, u32[]{:S(2)}, u32[]{:S(2)}) async-start(bf16[2,16,64]{2,0,1:T(2,128)(2,1)} %copy.103), calls=%async_computation.3 | async-start | bytes 16384 | tf_op jit(solution)/shard_map/all_to_all | solution.py:125
  113.9 12.3 %all-to-all-done.3 = bf16[2,16,64]{2,0,1:T(2,128)(2,1)S(1)} async-done(((bf16[2,16,64]{2,0,1:T(2,128)(2,1)}), bf16[2,16,64]{2,0,1:T(2,128)(2,1)S(1)}, u32[]{:S(2)}, u32[]{:S(2)}) %all-to-all-start.3) | async-done | bytes 4128 | tf_op jit(solution)/shard_map/all_to_all | solution.py:125
  126.2 36.9 %all-to-all-start.4 = ((bf16[4,64,1024]{2,0,1:T(4,128)(2,1)}), bf16[4,64,1024]{2,0,1:T(4,128)(2,1)S(1)}, u32[]{:S(2)}, u32[]{:S(2)}) async-start(bf16[4,64,1024]{2,0,1:T(4,128)(2,1)} %copy.105), calls=%async_computation.4 | async-start | bytes 1048576 | tf_op jit(solution)/shard_map/all_to_all | solution.py:74
  164.3 15.6 %all-to-all-done.4 = bf16[4,64,1024]{2,0,1:T(4,128)(2,1)S(1)} async-done(((bf16[4,64,1024]{2,0,1:T(4,128)(2,1)}), bf16[4,64,1024]{2,0,1:T(4,128)(2,1)S(1)}, u32[]{:S(2)}, u32[]{:S(2)}) %all-to-all-start.4) | async-done | bytes 524320 | tf_op jit(solution)/shard_map/all_to_all | solution.py:74
  179.9 3.7 %all-to-all-start.5 = ((bf16[4,64,1024]{2,0,1:T(4,128)(2,1)}), bf16[4,64,1024]{2,0,1:T(4,128)(2,1)S(1)}, u32[]{:S(2)}, u32[]{:S(2)}) async-start(bf16[4,64,1024]{2,0,1:T(4,128)(2,1)} %copy.107), calls=%async_computation.5 | async-start | bytes 1048576 | tf_op jit(solution)/shard_map/all_to_all | solution.py:75
  183.6 2.3 copy.122
  185.9 14.6 %all-to-all-done.5 = bf16[4,64,1024]{2,0,1:T(4,128)(2,1)S(1)} async-done(((bf16[4,64,1024]{2,0,1:T(4,128)(2,1)}), bf16[4,64,1024]{2,0,1:T(4,128)(2,1)S(1)}, u32[]{:S(2)}, u32[]{:S(2)}) %all-to-all-start.5) | async-done | bytes 524320 | tf_op jit(solution)/shard_map/all_to_all | solution.py:75
  201.3 3.7 %all-to-all-start.8 = ((bf16[4,64,1024]{2,0,1:T(4,128)(2,1)}), bf16[4,64,1024]{2,0,1:T(4,128)(2,1)S(1)}, u32[]{:S(2)}, u32[]{:S(2)}) async-start(bf16[4,64,1024]{2,0,1:T(4,128)(2,1)} %copy.122), calls=%async_computation.8 | async-start | bytes 1048576 | tf_op jit(solution)/shard_map/all_to_all | solution.py:76
  214.9 7.0 %all-to-all-done.8 = bf16[4,64,1024]{2,0,1:T(4,128)(2,1)S(1)} async-done(((bf16[4,64,1024]{2,0,1:T(4,128)(2,1)}), bf16[4,64,1024]{2,0,1:T(4,128)(2,1)S(1)}, u32[]{:S(2)}, u32[]{:S(2)}) %all-to-all-start.8) | async-done | bytes 524320 | tf_op jit(solution)/shard_map/all_to_all | solution.py:76
  221.9 3.7 %all-to-all-start.6 = ((bf16[128,2,8]{2,1,0:T(2,128)(2,1)}), bf16[128,2,8]{2,1,0:T(2,128)(2,1)S(1)}, u32[]{:S(2)}, u32[]{:S(2)}) async-start(bf16[128,2,8]{2,1,0:T(2,128)(2,1)} %copy.111), calls=%async_computation.6 | async-start | bytes 131072 | tf_op jit(solution)/shard_map/all_to_all | solution.py:102
  225.6 2.4 copy.117
  228.0 5.5 %all-to-all-done.6 = bf16[128,2,8]{2,1,0:T(2,128)(2,1)S(1)} async-done(((bf16[128,2,8]{2,1,0:T(2,128)(2,1)}), bf16[128,2,8]{2,1,0:T(2,128)(2,1)S(1)}, u32[]{:S(2)}, u32[]{:S(2)}) %all-to-all-start.6) | async-done | bytes 4128 | tf_op jit(solution)/shard_map/all_to_all | solution.py:102
  233.5 3.6 %all-to-all-start.7 = ((bf16[2,1024,128]{2,0,1:T(2,128)(2,1)}), bf16[2,1024,128]{2,0,1:T(2,128)(2,1)S(1)}, u32[]{:S(2)}, u32[]{:S(2)}) async-start(bf16[2,1024,128]{2,0,1:T(2,128)(2,1)} %copy.117), calls=%async_computation.7 | async-start | bytes 1048576 | tf_op jit(solution)/shard_map/all_to_all | solution.py:125
  239.8 2.5 fusion.28
  244.3 21.9 %all-to-all-done.7 = bf16[2,1024,128]{2,0,1:T(2,128)(2,1)S(1)} async-done(((bf16[2,1024,128]{2,0,1:T(2,128)(2,1)}), bf16[2,1024,128]{2,0,1:T(2,128)(2,1)S(1)}, u32[]{:S(2)}, u32[]{:S(2)}) %all-to-all-start.7) | async-done | bytes 524320 | tf_op jit(solution)/shard_map/all_to_all | solution.py:125
  266.2 9.2 %all-to-all-start.9 = ((bf16[128,2,1024]{2,1,0:T(2,128)(2,1)}), bf16[128,2,1024]{2,1,0:T(2,128)(2,1)S(1)}, u32[]{:S(2)}, u32[]{:S(2)}) async-start(bf16[128,2,1024]{2,1,0:T(2,128)(2,1)} %copy.126), calls=%async_computation.9 | async-start | bytes 1048576 | tf_op jit(solution)/shard_map/all_to_all | solution.py:101
  277.2 15.0 %all-to-all-done.9 = bf16[128,2,1024]{2,1,0:T(2,128)(2,1)S(1)} async-done(((bf16[128,2,1024]{2,1,0:T(2,128)(2,1)}), bf16[128,2,1024]{2,1,0:T(2,128)(2,1)S(1)}, u32[]{:S(2)}, u32[]{:S(2)}) %all-to-all-start.9) | async-done | bytes 524320 | tf_op jit(solution)/shard_map/all_to_all | solution.py:101
  (85 shorter events, 43.5 us)
Async XLA Ops:
  0.0 297.1 %copy-start = (bf16[1024,1024]{1,0:T(8,128)(2,1)S(1)}, bf16[1024,1024]{1,0:T(8,128)(2,1)}, u32[]{:S(2)}) copy-start(bf16[1024,1024]{1,0:T(8,128)(2,1)} %param.9) | copy-start | bytes 6291460
  0.0 20.5 %copy-start.3 = (bf16[4,64,1024]{2,1,0:T(8,128)(2,1)S(1)}, bf16[4,64,1024]{2,1,0:T(8,128)(2,1)}, u32[]{:S(2)}) copy-start(bf16[4,64,1024]{2,1,0:T(8,128)(2,1)} %param.8) | copy-start | bytes 1572868
  0.0 56.3 %copy-start.1 = (bf16[4,64,1024]{2,1,0:T(8,128)(2,1)S(1)}, bf16[4,64,1024]{2,1,0:T(8,128)(2,1)}, u32[]{:S(2)}) copy-start(bf16[4,64,1024]{2,1,0:T(8,128)(2,1)} %param.6) | copy-start | bytes 1572868
  2.3 45.4 %all-to-all-start.1 = ((bf16[32,64,128]{2,1,0:T(8,128)(2,1)}), bf16[32,64,128]{2,1,0:T(8,128)(2,1)}, u32[]{:S(2)}, u32[]{:S(2)}) async-start(bf16[32,64,128]{2,1,0:T(8,128)(2,1)} %bitcast.145), calls=%async_computation.1 | async-start | bytes 1048576 | tf_op jit(solution)/shard_map/all_to_all | solution.py:65
  47.7 29.0 %all-to-all-start.2 = ((bf16[32,64,128]{2,1,0:T(8,128)(2,1)}), bf16[32,64,128]{2,1,0:T(8,128)(2,1)S(1)}, u32[]{:S(2)}, u32[]{:S(2)}) async-start(bf16[32,64,128]{2,1,0:T(8,128)(2,1)} %bitcast.144), calls=%async_computation.2 | async-start | bytes 1048576 | tf_op jit(solution)/shard_map/all_to_all | solution.py:66
  76.7 21.8 %all-to-all-start = ((bf16[32,64,128]{2,1,0:T(8,128)(2,1)}), bf16[32,64,128]{2,1,0:T(8,128)(2,1)}, u32[]{:S(2)}, u32[]{:S(2)}) async-start(bf16[32,64,128]{2,1,0:T(8,128)(2,1)} %bitcast.143), calls=%async_computation | async-start | bytes 1048576 | tf_op jit(solution)/shard_map/all_to_all | solution.py:64
  100.4 62.7 %copy-start.2 = (bf16[4,64,1024]{2,1,0:T(8,128)(2,1)S(1)}, bf16[4,64,1024]{2,1,0:T(8,128)(2,1)}, u32[]{:S(2)}) copy-start(bf16[4,64,1024]{2,1,0:T(8,128)(2,1)} %param.7) | copy-start | bytes 1572868
  100.4 2.3 copy-start.6
  100.4 2.4 copy-start.7
  103.6 0.8 copy-start.8
  104.5 2.3 copy-start.6
  104.5 2.3 copy-start.7
  107.7 0.8 copy-start.8
  109.2 17.0 %all-to-all-start.3 = ((bf16[2,16,64]{2,0,1:T(2,128)(2,1)}), bf16[2,16,64]{2,0,1:T(2,128)(2,1)S(1)}, u32[]{:S(2)}, u32[]{:S(2)}) async-start(bf16[2,16,64]{2,0,1:T(2,128)(2,1)} %copy.103), calls=%async_computation.3 | async-start | bytes 16384 | tf_op jit(solution)/shard_map/all_to_all | solution.py:125
  126.2 53.7 %all-to-all-start.4 = ((bf16[4,64,1024]{2,0,1:T(4,128)(2,1)}), bf16[4,64,1024]{2,0,1:T(4,128)(2,1)S(1)}, u32[]{:S(2)}, u32[]{:S(2)}) async-start(bf16[4,64,1024]{2,0,1:T(4,128)(2,1)} %copy.105), calls=%async_computation.4 | async-start | bytes 1048576 | tf_op jit(solution)/shard_map/all_to_all | solution.py:74
  179.9 20.6 %all-to-all-start.5 = ((bf16[4,64,1024]{2,0,1:T(4,128)(2,1)}), bf16[4,64,1024]{2,0,1:T(4,128)(2,1)S(1)}, u32[]{:S(2)}, u32[]{:S(2)}) async-start(bf16[4,64,1024]{2,0,1:T(4,128)(2,1)} %copy.107), calls=%async_computation.5 | async-start | bytes 1048576 | tf_op jit(solution)/shard_map/all_to_all | solution.py:75
  200.5 0.8 copy-start.4
  201.3 20.6 %all-to-all-start.8 = ((bf16[4,64,1024]{2,0,1:T(4,128)(2,1)}), bf16[4,64,1024]{2,0,1:T(4,128)(2,1)S(1)}, u32[]{:S(2)}, u32[]{:S(2)}) async-start(bf16[4,64,1024]{2,0,1:T(4,128)(2,1)} %copy.122), calls=%async_computation.8 | async-start | bytes 1048576 | tf_op jit(solution)/shard_map/all_to_all | solution.py:76
  212.9 1.0 copy-start.5
  221.9 11.6 %all-to-all-start.6 = ((bf16[128,2,8]{2,1,0:T(2,128)(2,1)}), bf16[128,2,8]{2,1,0:T(2,128)(2,1)S(1)}, u32[]{:S(2)}, u32[]{:S(2)}) async-start(bf16[128,2,8]{2,1,0:T(2,128)(2,1)} %copy.111), calls=%async_computation.6 | async-start | bytes 131072 | tf_op jit(solution)/shard_map/all_to_all | solution.py:102
  233.5 32.7 %all-to-all-start.7 = ((bf16[2,1024,128]{2,0,1:T(2,128)(2,1)}), bf16[2,1024,128]{2,0,1:T(2,128)(2,1)S(1)}, u32[]{:S(2)}, u32[]{:S(2)}) async-start(bf16[2,1024,128]{2,0,1:T(2,128)(2,1)} %copy.117), calls=%async_computation.7 | async-start | bytes 1048576 | tf_op jit(solution)/shard_map/all_to_all | solution.py:125
  266.2 26.0 %all-to-all-start.9 = ((bf16[128,2,1024]{2,1,0:T(2,128)(2,1)}), bf16[128,2,1024]{2,1,0:T(2,128)(2,1)S(1)}, u32[]{:S(2)}, u32[]{:S(2)}) async-start(bf16[128,2,1024]{2,1,0:T(2,128)(2,1)} %copy.126), calls=%async_computation.9 | async-start | bytes 1048576 | tf_op jit(solution)/shard_map/all_to_all | solution.py:101
where the time goes:
time: 300 us; the launch traced here: 299 us
  waiting for transfers between devices  152 us (51%)
  starting transfers between devices  95.3 us (32%)
  local copies, waits for them, and re-layouts  35.6 us (12%)
  matrix products  11 us (4%)
  other arithmetic  3.95 us (1%)
    all_to_all x1, starting transfers between devices, column_attention(): lax.all_to_all(queries, 'row', split_axis=1, concat_axis=0, tiled=True)  36.9 us
    all_to_all x2, waiting for transfers between devices, body(): lax.all_to_all(for_sending(row_parts), 'col', split_axis=1, concat_axis=0...  34.2 us
    all_to_all x1, waiting for transfers between devices, row_attention(): lax.all_to_all(sent[1], 'col', split_axis=0, concat_axis=1, tiled=True)  26.1 us
    all_to_all x1, waiting for transfers between devices, row_attention(): lax.all_to_all(sent[2], 'col', split_axis=0, concat_axis=1, tiled=True)  19.4 us
    all_to_all x1, starting transfers between devices, row_attention(): lax.all_to_all(sent[1], 'col', split_axis=0, concat_axis=1, tiled=True)  18.3 us
    all_to_all x1, waiting for transfers between devices, column_attention(): lax.all_to_all(queries, 'row', split_axis=1, concat_axis=0, tiled=True)  15.6 us
    all_to_all x1, waiting for transfers between devices, column_attention(): lax.all_to_all(parts[0], 'row', split_axis=0, concat_axis=1, tiled=True)  15 us
    all_to_all x1, waiting for transfers between devices, row_attention(): lax.all_to_all(sent[0], 'col', split_axis=0, concat_axis=1, tiled=True)  14.8 us
  transfers between devices with their start and end apart: 10, of which 10 were waited for; matrix products, arithmetic and copies ran while one was open for 10% of the time, Pallas kernels for 0%

commit v1 on v0

v1 whole, which is shorter than its diff:
```python
import jax
import jax.numpy as jnp
from jax import lax
from jax.experimental import pallas as pl
from jax.experimental.pallas import tpu as pltpu
from jax.sharding import PartitionSpec as P

HEADS = 8
HEAD_DIM = 128
SCALE = HEAD_DIM**-0.5
BATCHES = 2
PER = 4 // BATCHES
GROUPS = 2 + BATCHES
BLOCK = 256
MASKED = -1e30
MESH = pl.DeviceIdType.MESH
NT = (((1,), (1,)), ((), ()))


def device(x, y, z, core):
    return (y * 8 + lax.rem(z, 4) * 2 + core, x * 4 + lax.div(z, 4))


def loop(first, last, step):
    def run(i, carry):
        step(i)
        return carry

    lax.fori_loop(first, last, run, 0)


def kernel(
    q_in,
    k_in,
    v_in,
    out,
    home_q,
    home_k,
    home_v,
    row_q,
    row_k,
    row_v,
    col_q,
    col_k,
    col_v,
    row_part,
    row_level,
    col_part,
    col_level,
    home_row_part,
    home_row_level,
    home_col_part,
    home_col_level,
    home_context,
    wide_q,
    wide_k,
    wide_v,
    wide_o,
    in_send,
    in_recv,
    row_send,
    row_recv,
    col_send,
    col_recv,
    row_back_send,
    row_back_recv,
    col_back_send,
    col_back_recv,
    out_send,
    out_recv,
):
    at_row, at_col = lax.axis_index("row"), lax.axis_index("col")
    y, z_lo, core = lax.div(at_row, 8), lax.rem(lax.div(at_row, 2), 4), lax.rem(at_row, 2)
    x, z_hi = lax.div(at_col, 4), lax.rem(at_col, 4)
    z = z_hi * 4 + z_lo
    near = lax.div(z, 2)
    active = lax.rem(z, 2) == 0
    me = y * 2 + core

    def peer_x(other):
        return device(other, y, z, core)

    def peer_yc(other):
        return device(x, lax.div(other, 2), z, lax.rem(other, 2))

    def peer_z(other):
        return device(x, y, other, core)

    def remote(src, dst, send, recv, to):
        return pltpu.make_async_remote_copy(
            src_ref=src, dst_ref=dst, send_sem=send, recv_sem=recv, device_id=to, device_id_type=MESH
        )

    barrier = pltpu.get_barrier_semaphore()

    def greet(to):
        pl.semaphore_signal(barrier, inc=1, device_id=to, device_id_type=MESH)

    @pl.when(active)
    def _():
        loop(1, 16, lambda d: greet(peer_z(lax.rem(z + d, 16))))
        loop(1, 4, lambda d: greet(peer_x(lax.rem(x + d, 4))))
        loop(1, 8, lambda d: greet(peer_yc(lax.rem(me + d, 8))))
        pl.semaphore_wait(barrier, 25)

    @pl.when(jnp.logical_not(active))
    def _():
        loop(0, 8, lambda h: greet(peer_z(h * 2)))
        pl.semaphore_wait(barrier, 8)

    def rows_of(group):
        return pl.ds(0, 4) if group < 2 else pl.ds((group - 2) * PER, PER)

    def of(group, key, value, query):
        return (key, value)[group] if group < 2 else query

    def in_copy(group, head):
        rows = rows_of(group)
        src = of(group, k_in, v_in, q_in).at[rows, :, pl.ds(pl.multiple_of(head * 128, 128), 128)]
        dst = in_slot(group, z)
        return remote(src, dst, in_send.at[group, head], in_recv.at[group, z], peer_z(head * 2))

    def in_slot(group, source):
        columns = pl.ds(pl.multiple_of(lax.div(source, 4) * 64, 64), 64)
        return of(group, home_k, home_v, home_q).at[lax.rem(source, 4), rows_of(group), columns, :]

    def in_own(group):
        src = of(group, k_in, v_in, q_in).at[rows_of(group), :, pl.ds(pl.multiple_of(near * 128, 128), 128)]
        return pltpu.make_async_copy(src, in_slot(group, z), in_recv.at[group, z])

    def in_start(group):
        @pl.when(active)
        def _():
            in_own(group).start()

        @pl.when(jnp.logical_not(active))
        def _():
            in_copy(group, near).start()

        loop(1, 8, lambda d: in_copy(group, lax.rem(near + d, 8)).start())

    def in_sent(group):
        @pl.when(jnp.logical_not(active))
        def _():
            in_copy(group, near).wait_send()

        loop(1, 8, lambda d: in_copy(group, lax.rem(near + d, 8)).wait_send())

    def in_wait(group):
        in_own(group).wait()

        def one(d):
            source = lax.rem(z + d, 16)
            slot = in_slot(group, source)
            remote(slot, slot, in_send.at[group, 0], in_recv.at[group, source], peer_z(source)).wait_recv()

        loop(1, 16, one)

    def row_slot(group, source):
        columns = pl.ds(pl.multiple_of(source * 256, 256), 256)
        return of(group, row_k, row_v, row_q).at[rows_of(group), columns, :]

    def row_copy(group, other):
        src = of(group, home_k, home_v, home_q).at[other, rows_of(group)]
        return remote(src, row_slot(group, x), row_send.at[group, other], row_recv.at[group, x], peer_x(other))

    def row_own(group):
        src = of(group, home_k, home_v, home_q).at[x, rows_of(group)]
        return pltpu.make_async_copy(src, row_slot(group, x), row_recv.at[group, x])

    def row_wait(group):
        row_own(group).wait()

        def one(d):
            source = lax.rem(x + d, 4)
            slot = row_slot(group, source)
            remote(slot, slot, row_send.at[group, source], row_recv.at[group, source], peer_x(source)).wait_recv()

        loop(1, 4, one)

    def col_slot(group, source):
        of_y, of_core = lax.div(source, 2), lax.rem(source, 2)
        if group < 2:
            return (col_k, col_v)[group].at[of_y, :, of_core]
        return col_q.at[group - 2, of_y, :, of_core]

    def col_source(group, other):
        columns = pl.ds(pl.multiple_of(other * 32, 32), 32)
        return of(group, home_k, home_v, home_q).at[:, rows_of(group), columns, :]

    def col_copy(group, other):
        return remote(
            col_source(group, other),
            col_slot(group, me),
            col_send.at[group, other],
            col_recv.at[group, me],
            peer_yc(other),
        )

    def col_own(group):
        return pltpu.make_async_copy(col_source(group, me), col_slot(group, me), col_recv.at[group, me])

    def col_wait(group):
        col_own(group).wait()

        def one(d):
            source = lax.rem(me + d, 8)
            slot = col_slot(group, source)
            remote(slot, slot, col_send.at[group, source], col_recv.at[group, source], peer_yc(source)).wait_recv()

        loop(1, 8, one)

    def spread(group):
        row_own(group).start()
        col_own(group).start()
        loop(1, 4, lambda d: row_copy(group, lax.rem(x + d, 4)).start())
        loop(1, 8, lambda d: col_copy(group, lax.rem(me + d, 8)).start())

    def spread_sent(group):
        loop(1, 4, lambda d: row_copy(group, lax.rem(x + d, 4)).wait_send())
        loop(1, 8, lambda d: col_copy(group, lax.rem(me + d, 8)).wait_send())

    def row_back(batch, other, source, target):
        rows = pl.ds(batch * PER, PER)
        columns = pl.ds(pl.multiple_of(target * 256, 256), 256)
        part = remote(
            row_part.at[rows, columns, :],
            home_row_part.at[source, rows],
            row_back_send.at[batch, 0, other],
            row_back_recv.at[batch, 0, source],
            peer_x(other),
        )
        level = remote(
            row_level.at[batch, columns, :],
            home_row_level.at[batch, source],
            row_back_send.at[batch, 1, other],
            row_back_recv.at[batch, 1, source],
            peer_x(other),
        )
        return part, level

    def row_back_own(batch):
        rows = pl.ds(batch * PER, PER)
        columns = pl.ds(pl.multiple_of(x * 256, 256), 256)
        return (
            pltpu.make_async_copy(
                row_part.at[rows, columns, :], home_row_part.at[x, rows], row_back_recv.at[batch, 0, x]
            ),
            pltpu.make_async_copy(
                row_level.at[batch, columns, :], home_row_level.at[batch, x], row_back_recv.at[batch, 1, x]
            ),
        )

    def col_back(batch, other, source, target):
        rows = pl.ds(batch * PER, PER)
        columns = pl.ds(pl.multiple_of(source * 32, 32), 32)
        part = remote(
            col_part.at[batch, lax.div(target, 2), :, lax.rem(target, 2)],
            home_col_part.at[:, rows, columns, :],
            col_back_send.at[batch, 0, other],
            col_back_recv.at[batch, 0, source],
            peer_yc(other),
        )
        level = remote(
            col_level.at[batch],
            home_col_level.at[batch, columns, :],
            col_back_send.at[batch, 1, other],
            col_back_recv.at[batch, 1, source],
            peer_yc(other),
        )
        return part, level

    def col_back_own(batch):
        rows = pl.ds(batch * PER, PER)
        columns = pl.ds(pl.multiple_of(me * 32, 32), 32)
        return (
            pltpu.make_async_copy(
                col_part.at[batch, y, :, core],
                home_col_part.at[:, rows, columns, :],
                col_back_recv.at[batch, 0, me],
            ),
            pltpu.make_async_copy(
                col_level.at[batch], home_col_level.at[batch, columns, :], col_back_recv.at[batch, 1, me]
            ),
        )

    def start_both(pair):
        for copy in pair:
            copy.start()

    def row_return(batch):
        start_both(row_back_own(batch))

        def one(d):
            other = lax.rem(x + d, 4)
            start_both(row_back(batch, other, x, other))

        loop(1, 4, one)

    def col_return(batch):
        start_both(col_back_own(batch))

        def one(d):
            other = lax.rem(me + d, 8)
            start_both(col_back(batch, other, me, other))

        loop(1, 8, one)

    def return_wait(batch):
        for copy in row_back_own(batch) + col_back_own(batch):
            copy.wait()

        def one_row(d):
            other = lax.rem(x + d, 4)
            for copy in row_back(batch, other, other, x):
                copy.wait_recv()

        def one_col(d):
            other = lax.rem(me + d, 8)
            for copy in col_back(batch, other, other, me):
                copy.wait_recv()

        loop(1, 4, one_row)
        loop(1, 8, one_col)

    def return_sent(batch):
        def one_row(d):
            other = lax.rem(x + d, 4)
            for copy in row_back(batch, other, x, other):
                copy.wait_send()

        def one_col(d):
            other = lax.rem(me + d, 8)
            for copy in col_back(batch, other, me, other):
                copy.wait_send()

        loop(1, 4, one_row)
        loop(1, 8, one_col)

    def out_slot(batch, head):
        return out.at[pl.ds(batch * PER, PER), :, pl.ds(pl.multiple_of(head * 128, 128), 128)]

    def out_source(batch, other):
        columns = pl.ds(pl.multiple_of(lax.div(other, 4) * 64, 64), 64)
        return home_context.at[lax.rem(other, 4), pl.ds(batch * PER, PER), columns, :]

    def out_copy(batch, other):
        return remote(
            out_source(batch, other),
            out_slot(batch, near),
            out_send.at[batch, other],
            out_recv.at[batch, near],
            peer_z(other),
        )

    def out_own(batch):
        return pltpu.make_async_copy(out_source(batch, z), out_slot(batch, near), out_recv.at[batch, near])

    def out_start(batch):
        out_own(batch).start()
        loop(1, 16, lambda d: out_copy(batch, lax.rem(z + d, 16)).start())

    def out_sent(batch):
        loop(1, 16, lambda d: out_copy(batch, lax.rem(z + d, 16)).wait_send())

    def out_arrived(batch):
        def one(head):
            slot = out_slot(batch, head)
            remote(slot, slot, out_send.at[batch, 0], out_recv.at[batch, head], peer_z(head * 2)).wait_recv()

        @pl.when(active)
        def _():
            out_own(batch).wait()

        @pl.when(jnp.logical_not(active))
        def _():
            one(near)

        loop(1, 8, lambda d: one(lax.rem(near + d, 8)))

    def row_work(batch):
        row_level[batch] = jnp.zeros((1024, 128), jnp.bfloat16)
        lane = lax.broadcasted_iota(jnp.int32, (BLOCK, 128), 1)
        causal = lax.broadcasted_iota(jnp.int32, (BLOCK, BLOCK), 0) >= lax.broadcasted_iota(
            jnp.int32, (BLOCK, BLOCK), 1
        )

        def one(step):
            r = batch * PER + step
            mark = (y * 8 + x * 2 + core) * PER + step
            for at in range(1024 // BLOCK):
                here = pl.ds(at * BLOCK, BLOCK)
                query = row_q[r, here]
                scores = lax.dot_general(
                    query, row_k[r, pl.ds(0, (at + 1) * BLOCK)], NT, preferred_element_type=jnp.float32
                )
                last = jnp.where(causal, scores[:, at * BLOCK :], MASKED)
                scores = jnp.concatenate([scores[:, : at * BLOCK], last], axis=1) if at else last
                best = jnp.max(scores, axis=1, keepdims=True)
                weights = jnp.exp((scores - best) * SCALE)
                total = jnp.maximum(jnp.sum(weights, axis=1, keepdims=True), 1.0)
                summed = jnp.dot(
                    weights.astype(jnp.bfloat16),
                    row_v[r, pl.ds(0, (at + 1) * BLOCK)],
                    preferred_element_type=jnp.float32,
                )
                row_part[r, here] = (summed / total).astype(jnp.bfloat16)
                level = (best * SCALE + jnp.log(total)).astype(jnp.bfloat16).astype(jnp.float32)
                old = row_level[batch, here].astype(jnp.float32)
                row_level[batch, here] = jnp.where(lane == mark, level, old).astype(jnp.bfloat16)

        loop(0, PER, one)

    def widen(target, source, rows):
        def one(block):
            of_y, of_z, of_core = lax.div(block, 8), lax.rem(lax.div(block, 2), 4), lax.rem(block, 2)
            piece = source[of_y, of_z, of_core].astype(jnp.float32).reshape(rows * 32, 128)
            target[pl.ds(pl.multiple_of(block * rows * 32, 32), rows * 32)] = piece

        loop(0, 32, one)

    def col_work(batch):
        queries = 32 * PER
        widen(wide_q, col_q.at[batch], PER)
        at = lax.broadcasted_iota(jnp.int32, (queries, 128), 0)
        lane = lax.broadcasted_iota(jnp.int32, (queries, 128), 1)
        lower = lax.div(at, PER) * 4 + batch * PER + lax.rem(at, PER) > lane

        def one(c, levels):
            query = wide_q[pl.ds(c, queries, stride=32), :].astype(jnp.bfloat16)
            key = wide_k[pl.ds(c, 128, stride=32), :].astype(jnp.bfloat16)
            value = wide_v[pl.ds(c, 128, stride=32), :].astype(jnp.bfloat16)
            scores = lax.dot_general(query, key, NT, preferred_element_type=jnp.float32) * SCALE
            best = jnp.max(jnp.where(lower, scores, MASKED), axis=1, keepdims=True)
            weights = jnp.where(lower, jnp.exp(scores - best), 0.0)
            total = jnp.maximum(jnp.sum(weights, axis=1, keepdims=True), 1.0)
            summed = jnp.dot(weights.astype(jnp.bfloat16), value, preferred_element_type=jnp.float32)
            wide_o[pl.ds(c, queries, stride=32), :] = summed / total
            return jnp.where(lane == c, best + jnp.log(total), levels)

        levels = lax.fori_loop(0, 32, one, jnp.zeros((queries, 128), jnp.float32), unroll=4)
        levels = jnp.concatenate([levels, jnp.zeros((128 - queries, 128), jnp.float32)], axis=0)
        col_level[batch] = levels.T[:32].astype(jnp.bfloat16)

        def narrow(block):
            of_y, of_z, of_core = lax.div(block, 8), lax.rem(lax.div(block, 2), 4), lax.rem(block, 2)
            piece = wide_o[pl.ds(pl.multiple_of(block * PER * 32, 32), PER * 32)]
            col_part[batch, of_y, of_z, of_core] = piece.astype(jnp.bfloat16).reshape(PER, 32, 128)

        loop(0, 32, narrow)

    def combine(batch):
        row_levels = home_row_level[batch, 0].astype(jnp.float32)
        for source in range(1, 4):
            row_levels = row_levels + home_row_level[batch, source].astype(jnp.float32)
        col_levels = home_col_level[batch].astype(jnp.float32)
        top = jnp.maximum(row_levels, col_levels)
        row_factor = jnp.exp(row_levels - top)
        col_factor = jnp.exp(col_levels - top)
        denom = row_factor + col_factor
        shift = lax.rem(128 - (y * 8 + core) * PER, 128)
        row_factor = pltpu.roll(row_factor / denom, shift, 1)
        col_factor = pltpu.roll(col_factor / denom, shift, 1)
        for source in range(4):
            for step in range(PER):
                lane = source * 2 * PER + step
                r = batch * PER + step
                home_context[source, r] = (
                    row_factor[:, lane : lane + 1] * home_row_part[source, r].astype(jnp.float32)
                    + col_factor[:, lane : lane + 1] * home_col_part[source, r].astype(jnp.float32)
                ).astype(jnp.bfloat16)

    in_start(0)
    in_start(1)
    for batch in range(BATCHES):
        if batch < 2:
            in_sent(batch)
        in_start(2 + batch)

        if batch < 2:

            @pl.when(active)
            def _(batch=batch):
                in_wait(batch)
                spread(batch)

    @pl.when(active)
    def _():
        for batch in range(BATCHES):
            in_wait(2 + batch)
            spread(2 + batch)
            if batch > 0:
                return_wait(batch - 1)
                combine(batch - 1)
                out_start(batch - 1)
            if batch == 0:
                row_wait(0)
                row_wait(1)
            row_wait(2 + batch)
            row_work(batch)
            row_return(batch)
            if batch == 0:
                col_wait(0)
                widen(wide_k, col_k, 4)
                col_wait(1)
                widen(wide_v, col_v, 4)
            col_wait(2 + batch)
            col_work(batch)
            col_return(batch)
        return_wait(BATCHES - 1)
        combine(BATCHES - 1)
        out_start(BATCHES - 1)
        for group in range(GROUPS):
            spread_sent(group)
        for batch in range(BATCHES):
            return_sent(batch)
            out_sent(batch)

    for batch in range(BATCHES):
        in_sent(2 + batch)
    for batch in range(BATCHES):
        out_arrived(batch)


def attention(queries, key_vectors, values):
    bf16, f32 = jnp.bfloat16, jnp.float32
    dma = pltpu.SemaphoreType.DMA
    home = pltpu.VMEM((4, 4, 256, 128), bf16)
    rows = pltpu.VMEM((4, 1024, 128), bf16)
    batches = pltpu.VMEM((BATCHES, 4, 4, 2, PER, 32, 128), bf16)
    columns = pltpu.VMEM((4, 4, 2, 4, 32, 128), bf16)
    anywhere = pl.BlockSpec(memory_space=pl.ANY)
    return pl.pallas_call(
        kernel,
        out_shape=jax.ShapeDtypeStruct(queries.shape, bf16),
        in_specs=[anywhere] * 3,
        out_specs=anywhere,
        scratch_shapes=[
            home,
            home,
            home,
            rows,
            rows,
            rows,
            batches,
            columns,
            columns,
            rows,
            pltpu.VMEM((BATCHES, 1024, 128), bf16),
            batches,
            pltpu.VMEM((BATCHES, 32, 128), bf16),
            home,
            pltpu.VMEM((BATCHES, 4, 256, 128), bf16),
            home,
            pltpu.VMEM((BATCHES, 256, 128), bf16),
            home,
            pltpu.VMEM((32 * PER * 32, 128), f32),
            pltpu.VMEM((4096, 128), f32),
            pltpu.VMEM((4096, 128), f32),
            pltpu.VMEM((32 * PER * 32, 128), f32),
            dma((GROUPS, 8)),
            dma((GROUPS, 16)),
            dma((GROUPS, 4)),
            dma((GROUPS, 4)),
            dma((GROUPS, 8)),
            dma((GROUPS, 8)),
            dma((BATCHES, 2, 4)),
            dma((BATCHES, 2, 4)),
            dma((BATCHES, 2, 8)),
            dma((BATCHES, 2, 8)),
            dma((BATCHES, 16)),
            dma((BATCHES, 8)),
        ],
        compiler_params=pltpu.CompilerParams(
            collective_id=0, has_side_effects=True, vmem_limit_bytes=48 * 1024 * 1024
        ),
    )(queries, key_vectors, values)


def body(queries, key_vectors, values, out_weight):
    rows_dev, cols_dev, width = queries.shape
    context = attention(queries, key_vectors, values)
    flat = context.reshape(rows_dev * cols_dev, width)
    attended = jnp.dot(flat, out_weight, preferred_element_type=jnp.float32).astype(jnp.bfloat16)
    return attended.reshape(rows_dev, cols_dev, width)


def solution(mesh):
    in_specs = (P("row", "col", None), P("row", "col", None), P("row", "col", None), P())
    out_specs = P("row", "col", None)
    return jax.shard_map(body, mesh=mesh, in_specs=in_specs, out_specs=out_specs, check_vma=False)
```

time: 300 us -> 180 us (0.60)
  Pallas kernels: 0 us -> 174 us
  waiting for transfers between devices: 152 us -> 0 us
  starting transfers between devices: 95.3 us -> 0 us
  local copies, waits for them, and re-layouts: 35.6 us -> 3.28 us
  matrix products: 11 us -> 1.51 us
  other arithmetic: 3.95 us -> 0 us
    pallas_call x0 -> x1, Pallas kernels: none -> 174 us  [attention(): pl.pallas_call(kernel, out_shape=jax.ShapeDtypeStruct(queries.shape, bf16...]
    all_to_all x10 -> x0, waiting for transfers between devices: 152 us -> none  [the longest x2 34.2 us: body(): lax.all_to_all(for_sending(row_parts), 'col', split_axis=1, concat_axis=0...]
    all_to_all x10 -> x0, starting transfers between devices: 95.3 us -> none  [the longest x1 36.9 us: column_attention(): lax.all_to_all(queries, 'row', split_axis=1, concat_axis=0, tiled=True)]
    all_to_all x10 -> x0, local copies, waits for them, and re-layouts: 9.62 us -> none  [the longest x1 1.89 us: row_attention(): lax.all_to_all(sent[1], 'col', split_axis=0, concat_axis=1, tiled=True)]
    dot_general x6 -> x0, matrix products: 9.54 us -> none  [the longest x2 3.69 us: one_item(): jnp.einsum('jd,kd->jk', query_rows, key_rows, preferred_element_type=jnp....]
    reshape x4 -> x0, local copies, waits for them, and re-layouts: 6.69 us -> none  [the longest x1 2.17 us: column_attention(): query_cols.reshape(shape_four)]
    unnamed x18 -> x8, local copies, waits for them, and re-layouts: 7.95 us -> 3.28 us
    convert_element_type x10 -> x0, local copies, waits for them, and re-layouts: 4.42 us -> none  [the longest x2 1.89 us: combine(): second_part.astype(jnp.float32)]
  transfers between devices with their start and end apart: 10 -> 0, of which waited for: 10 -> 0; matrix products, arithmetic and copies ran while one was open for 10% -> 0% of each run, Pallas kernels for 0% -> 0%
where the time goes in v1:
time: 180 us; the launch traced here: 179 us
  Pallas kernels  174 us (97%)
  local copies, waits for them, and re-layouts  3.28 us (2%)
    pallas_call x1, Pallas kernels, attention(): pl.pallas_call(kernel, out_shape=jax.ShapeDtypeStruct(queries.shape, bf16...  174 us

profile of v1, /device:TPU:1, one launch (start us, length us, event | category | flops | bytes accessed | tf_op | source)
XLA Modules:
  0.0 178.6 jit_solution(17153861465243888137)
XLA Ops:
  0.0 0.0 copy-start
  0.0 0.0 copy-start.1
  0.0 1.2 copy-done.1
  1.2 0.0 copy-start.2
  1.2 1.0 copy-done.2
  2.2 0.0 copy-start.3
  2.2 1.0 copy-done.3
  3.3 173.8 %shard_map.46 = bf16[4,64,1024]{2,1,0:T(8,128)(2,1)S(1)} custom-call(bf16[4,64,1024]{2,1,0:T(8,128)(2,1)S(1)} %copy-done.1, bf16[4,64,1024]{2,1,0:T(8,128)(2,1)S(1)} %copy-done.2, bf16[4,64,1024]{2,1,0:T(8,128)(2,1)S(1)} %copy-done.3), custom_call_target="tpu_custom_call" | custom-call | tf_op jit(solution)/shard_map/pallas_call | solution.py:533
  177.1 0.0 copy-done
  177.1 1.5 convolution_convert_fusion
Async XLA Ops:
  0.0 177.1 %copy-start = (bf16[1024,1024]{1,0:T(8,128)(2,1)S(1)}, bf16[1024,1024]{1,0:T(8,128)(2,1)}, u32[]{:S(2)}) copy-start(bf16[1024,1024]{1,0:T(8,128)(2,1)} %param.7) | copy-start | bytes 6291460
  0.0 1.2 copy-start.1
  1.2 1.0 copy-start.2
  2.2 1.0 copy-start.3

commit v2 on v0

v2 whole, which is shorter than its diff:
```python
import jax
import jax.numpy as jnp
from jax import lax
from jax.experimental import pallas as pl
from jax.experimental.pallas import tpu as pltpu
from jax.sharding import PartitionSpec as P

HEADS = 8
HEAD_DIM = 128
SCALE = HEAD_DIM**-0.5
BATCHES = 4
PER = 4 // BATCHES
GROUPS = 2 + BATCHES
BLOCK = 256
MASKED = -1e30
MESH = pl.DeviceIdType.MESH
NT = (((1,), (1,)), ((), ()))


def device(x, y, z, core):
    return (y * 8 + lax.rem(z, 4) * 2 + core, x * 4 + lax.div(z, 4))


NEAREST = (0, 1, 7, 2, 6, 3, 5, 4)


def loop(first, last, step, unroll=1):
    def run(i, carry):
        step(i)
        return carry

    lax.fori_loop(first, last, run, 0, unroll=unroll)


def widen(source, target, per):
    def one(block):
        of_z, of_me = lax.div(block, 8), lax.rem(block, 8)
        piece = source[lax.div(of_me, 2), of_z, lax.rem(of_me, 2)]
        target[pl.ds(pl.multiple_of(block * per * 32, 32), per * 32)] = piece.astype(jnp.float32).reshape(
            per * 32, 128
        )

    loop(0, 32, one, 4)


def by_column(source, wide, target):
    widen(source, wide, 4)

    def one(c):
        target[c] = wide[pl.ds(c, 128, stride=32), :].astype(jnp.bfloat16)

    loop(0, 32, one, 8)


def row_item(query_ref, key_ref, value_ref, part_ref, level_ref, step):
    causal = lax.broadcasted_iota(jnp.int32, (BLOCK, BLOCK), 0) >= lax.broadcasted_iota(
        jnp.int32, (BLOCK, BLOCK), 1
    )
    first = (lax.broadcasted_iota(jnp.int32, (16, 128), 1) == 0).astype(jnp.bfloat16)
    for at in range(1024 // BLOCK):
        here, upto = pl.ds(at * BLOCK, BLOCK), pl.ds(0, (at + 1) * BLOCK)
        scores = lax.dot_general(query_ref[here], key_ref[upto], NT, preferred_element_type=jnp.float32)
        last = jnp.where(causal, scores[:, at * BLOCK :], MASKED)
        scores = jnp.concatenate([scores[:, : at * BLOCK], last], axis=1) if at else last
        best = jnp.max(scores, axis=1, keepdims=True)
        weights = jnp.exp((scores - best) * SCALE)
        total = jnp.maximum(jnp.sum(weights, axis=1, keepdims=True), 1.0)
        summed = jnp.dot(weights.astype(jnp.bfloat16), value_ref[upto], preferred_element_type=jnp.float32)
        part_ref[here] = (summed * (1.0 / total)).astype(jnp.bfloat16)
        level = jnp.broadcast_to(best * SCALE + jnp.log(total), (BLOCK, 128)).astype(jnp.bfloat16)
        turned = lax.dot_general(first, level, NT, preferred_element_type=jnp.float32)
        level_ref[step:, here] = turned[: level_ref.shape[0] - step]


def col_scores(query_ref, wide, key_by_col, scores, per):
    widen(query_ref, wide, per)

    def one(c):
        query = wide[pl.ds(c, 32 * per, stride=32), :].astype(jnp.bfloat16)
        scores[c] = lax.dot_general(query, key_by_col[c], NT, preferred_element_type=jnp.float32)

    loop(0, 32, one, 8)


def col_weights(scores, weights, inverse, level_ref, batch, per):
    queries = 32 * per
    at = lax.broadcasted_iota(jnp.int32, (queries, 128), 0)
    lane = lax.broadcasted_iota(jnp.int32, (queries, 128), 1)

    def grid_row(block, r):
        return lax.div(lax.rem(block, 8), 2) * 32 + lax.div(block, 8) * 8 + lax.rem(block, 2) * 4 + r

    lower = grid_row(lax.div(at, per), batch * per + lax.rem(at, per)) > grid_row(lax.div(lane, 4), lax.rem(lane, 4))

    def one(c, levels):
        masked = jnp.where(lower, scores[c], MASKED)
        best = jnp.max(masked, axis=1, keepdims=True)
        weight = jnp.where(lower, jnp.exp((masked - best) * SCALE), 0.0)
        total = jnp.maximum(jnp.sum(weight, axis=1, keepdims=True), 1.0)
        weights[c] = weight.astype(jnp.bfloat16)
        inverse[c] = jnp.broadcast_to(1.0 / total, (queries, 128))
        return jnp.where(lane == c, best * SCALE + jnp.log(total), levels)

    levels = lax.fori_loop(0, 32, one, jnp.zeros((queries, 128), jnp.float32), unroll=8)
    if queries < 128:
        levels = jnp.concatenate([levels, jnp.zeros((128 - queries, 128), jnp.float32)], axis=0)
    level_ref[...] = levels.T[:32].astype(jnp.bfloat16)


def col_sums(weights, inverse, value_by_col, wide, part_ref, per):
    def one(c):
        summed = jnp.dot(weights[c], value_by_col[c], preferred_element_type=jnp.float32)
        wide[pl.ds(c, 32 * per, stride=32), :] = summed * inverse[c]

    loop(0, 32, one, 8)

    def narrow(block):
        of_z, of_me = lax.div(block, 8), lax.rem(block, 8)
        piece = wide[pl.ds(pl.multiple_of(block * per * 32, 32), per * 32)]
        part_ref[lax.div(of_me, 2), of_z, lax.rem(of_me, 2)] = piece.astype(jnp.bfloat16).reshape(per, 32, 128)

    loop(0, 32, narrow, 4)


def combine(row_levels, row_parts, col_levels, col_parts, contexts, batch, shift, per):
    stacked = jnp.concatenate([row_levels[source] for source in range(4)], axis=0)
    if 32 * per < 128:
        stacked = jnp.concatenate([stacked, jnp.zeros((128 - 32 * per, 256), jnp.float32)], axis=0)
    row_level = stacked.T
    col_level = pltpu.roll(col_levels[...].astype(jnp.float32), shift, 1)
    top = jnp.maximum(row_level, col_level)
    row_factor = jnp.exp(row_level - top)
    col_factor = jnp.exp(col_level - top)
    inverse = 1.0 / (row_factor + col_factor)
    row_factor, col_factor = row_factor * inverse, col_factor * inverse
    for source in range(4):
        for step in range(per):
            lane = source * 8 * per + step
            r = batch * per + step
            contexts[source, r] = (
                row_factor[:, lane : lane + 1] * row_parts[source, r].astype(jnp.float32)
                + col_factor[:, lane : lane + 1] * col_parts[source, r].astype(jnp.float32)
            ).astype(jnp.bfloat16)


def kernel(
    q_in,
    k_in,
    v_in,
    out,
    home_q,
    home_k,
    home_v,
    row_q,
    row_k,
    row_v,
    col_q,
    col_k,
    col_v,
    row_part,
    row_level,
    col_part,
    col_level,
    home_row_part,
    home_row_level,
    home_col_part,
    home_col_level,
    home_context,
    key_by_col,
    value_by_col,
    wide,
    wide_q,
    wide_o,
    scores,
    weights,
    inverse,
    in_send,
    in_recv,
    row_send,
    row_recv,
    col_send,
    col_recv,
    row_back_send,
    row_back_recv,
    col_back_send,
    col_back_recv,
    out_send,
    out_recv,
):
    at_row, at_col = lax.axis_index("row"), lax.axis_index("col")
    y, z_lo, core = lax.div(at_row, 8), lax.rem(lax.div(at_row, 2), 4), lax.rem(at_row, 2)
    x, z_hi = lax.div(at_col, 4), lax.rem(at_col, 4)
    z = z_hi * 4 + z_lo
    near = lax.div(z, 2)
    active = lax.rem(z, 2) == 0
    me = y * 2 + core

    def peer_x(other):
        return device(other, y, z, core)

    def peer_yc(other):
        return device(x, lax.div(other, 2), z, lax.rem(other, 2))

    def peer_z(other):
        return device(x, y, other, core)

    def remote(src, dst, send, recv, to):
        return pltpu.make_async_remote_copy(
            src_ref=src, dst_ref=dst, send_sem=send, recv_sem=recv, device_id=to, device_id_type=MESH
        )

    def await_bytes(ref, semaphore):
        pltpu.make_async_copy(ref, ref, semaphore).wait()

    def others(mine, count, step):
        for offset in range(1, count):
            step(lax.rem(mine + offset, count))

    barrier = pltpu.get_barrier_semaphore()

    def greet(to):
        pl.semaphore_signal(barrier, inc=1, device_id=to, device_id_type=MESH)

    @pl.when(active)
    def _():
        others(z, 16, lambda other: greet(peer_z(other)))
        others(x, 4, lambda other: greet(peer_x(other)))
        others(me, 8, lambda other: greet(peer_yc(other)))
        pl.semaphore_wait(barrier, 25)

    @pl.when(jnp.logical_not(active))
    def _():
        for head in range(HEADS):
            greet(peer_z(head * 2))
        pl.semaphore_wait(barrier, 8)

    def rows_of(group):
        return pl.ds(0, 4) if group < 2 else pl.ds((group - 2) * PER, PER)

    def of(group, key, value, query):
        return (key, value)[group] if group < 2 else query

    def in_copy(group, head):
        rows = rows_of(group)
        src = of(group, k_in, v_in, q_in).at[rows, :, pl.ds(pl.multiple_of(head * 128, 128), 128)]
        dst = in_slot(group, z)
        return remote(src, dst, in_send.at[group, head], in_recv.at[group], peer_z(head * 2))

    def in_slot(group, source):
        columns = pl.ds(pl.multiple_of(lax.div(source, 4) * 64, 64), 64)
        return of(group, home_k, home_v, home_q).at[lax.rem(source, 4), rows_of(group), columns, :]

    def in_own(group):
        src = of(group, k_in, v_in, q_in).at[rows_of(group), :, pl.ds(pl.multiple_of(near * 128, 128), 128)]
        return pltpu.make_async_copy(src, in_slot(group, z), in_recv.at[group])

    def in_step(group, offset, before):
        head = lax.rem(near + offset, 8)

        def go():
            if before is not None:
                in_copy(before, head).wait_send()
            if group is not None:
                in_copy(group, head).start()

        if offset:
            go()
        else:

            @pl.when(active)
            def _():
                if group is not None:
                    in_own(group).start()

            @pl.when(jnp.logical_not(active))
            def _():
                go()

    def in_start(group):
        for offset in reversed(NEAREST):
            in_step(group, offset, None)

    def in_next(group):
        for offset in NEAREST:
            in_step(group + 1, offset, group)

    def in_sent(group):
        for offset in NEAREST:
            in_step(None, offset, group)

    def in_wait(group):
        await_bytes(of(group, home_k, home_v, home_q).at[:, rows_of(group)], in_recv.at[group])

    def row_slot(group, source):
        columns = pl.ds(pl.multiple_of(source * 256, 256), 256)
        return of(group, row_k, row_v, row_q).at[rows_of(group), columns, :]

    def row_copy(group, other):
        src = of(group, home_k, home_v, home_q).at[other, rows_of(group)]
        return remote(src, row_slot(group, x), row_send.at[group], row_recv.at[group], peer_x(other))

    def row_own(group):
        src = of(group, home_k, home_v, home_q).at[x, rows_of(group)]
        return pltpu.make_async_copy(src, row_slot(group, x), row_recv.at[group])

    def row_wait(group):
        await_bytes(of(group, row_k, row_v, row_q).at[rows_of(group)], row_recv.at[group])

    def col_slot(group, source):
        of_y, of_core = lax.div(source, 2), lax.rem(source, 2)
        if group < 2:
            return (col_k, col_v)[group].at[of_y, :, of_core]
        return col_q.at[group - 2, of_y, :, of_core]

    def col_source(group, other):
        columns = pl.ds(pl.multiple_of(other * 32, 32), 32)
        return of(group, home_k, home_v, home_q).at[:, rows_of(group), columns, :]

    def col_copy(group, other):
        return remote(
            col_source(group, other), col_slot(group, me), col_send.at[group], col_recv.at[group], peer_yc(other)
        )

    def col_own(group):
        return pltpu.make_async_copy(col_source(group, me), col_slot(group, me), col_recv.at[group])

    def col_wait(group):
        await_bytes((col_k, col_v)[group] if group < 2 else col_q.at[group - 2], col_recv.at[group])

    def spread(group):
        others(x, 4, lambda other: row_copy(group, other).start())
        others(me, 8, lambda other: col_copy(group, other).start())
        row_own(group).start()
        col_own(group).start()

    def spread_sent(group):
        home = of(group, home_k, home_v, home_q)
        await_bytes(home.at[pl.ds(0, 3), rows_of(group)], row_send.at[group])
        await_bytes(home.at[:, rows_of(group), pl.ds(0, 224), :], col_send.at[group])

    def row_back(batch, other, copy):
        rows = pl.ds(batch * PER, PER)
        columns = pl.ds(pl.multiple_of(other * 256, 256), 256)
        copy(
            row_part.at[rows, columns, :],
            home_row_part.at[x, rows],
            row_back_send.at[batch, 0],
            row_back_recv.at[batch, 0],
        )
        copy(
            row_level.at[batch, :, columns],
            home_row_level.at[batch, x],
            row_back_send.at[batch, 1],
            row_back_recv.at[batch, 1],
        )

    def col_back(batch, other, copy):
        columns = pl.ds(pl.multiple_of(me * 32, 32), 32)
        copy(
            col_part.at[batch, lax.div(other, 2), :, lax.rem(other, 2)],
            home_col_part.at[:, pl.ds(batch * PER, PER), columns, :],
            col_back_send.at[batch, 0],
            col_back_recv.at[batch, 0],
        )
        copy(
            col_level.at[batch],
            home_col_level.at[batch, columns, :],
            col_back_send.at[batch, 1],
            col_back_recv.at[batch, 1],
        )

    def send_to(device_id):
        return lambda src, dst, send, recv: remote(src, dst, send, recv, device_id).start()

    def keep(src, dst, send, recv):
        pltpu.make_async_copy(src, dst, recv).start()

    def row_return(batch):
        others(x, 4, lambda other: row_back(batch, other, send_to(peer_x(other))))
        row_back(batch, x, keep)

    def col_return(batch):
        others(me, 8, lambda other: col_back(batch, other, send_to(peer_yc(other))))
        col_back(batch, me, keep)

    def return_wait(batch):
        rows = pl.ds(batch * PER, PER)
        await_bytes(home_row_part.at[:, rows], row_back_recv.at[batch, 0])
        await_bytes(home_row_level.at[batch], row_back_recv.at[batch, 1])
        await_bytes(home_col_part.at[:, rows], col_back_recv.at[batch, 0])
        await_bytes(home_col_level.at[batch], col_back_recv.at[batch, 1])

    def return_sent(batch):
        rows = pl.ds(batch * PER, PER)
        await_bytes(row_part.at[rows, pl.ds(0, 768), :], row_back_send.at[batch, 0])
        await_bytes(row_level.at[batch, :, pl.ds(0, 768)], row_back_send.at[batch, 1])
        await_bytes(home_col_part.at[:, rows, pl.ds(0, 224), :], col_back_send.at[batch, 0])
        await_bytes(home_col_level.at[batch, pl.ds(0, 224), :], col_back_send.at[batch, 1])

    def out_slot(batch, head):
        return out.at[pl.ds(batch * PER, PER), :, pl.ds(pl.multiple_of(head * 128, 128), 128)]

    def out_source(batch, other):
        columns = pl.ds(pl.multiple_of(lax.div(other, 4) * 64, 64), 64)
        return home_context.at[lax.rem(other, 4), pl.ds(batch * PER, PER), columns, :]

    def out_copy(batch, other):
        return remote(
            out_source(batch, other), out_slot(batch, near), out_send.at[batch], out_recv.at[batch], peer_z(other)
        )

    def out_start(batch):
        others(z, 16, lambda other: out_copy(batch, other).start())
        pltpu.make_async_copy(out_source(batch, z), out_slot(batch, near), out_recv.at[batch]).start()

    def out_sent(batch):
        await_bytes(row_part.at[pl.ds(batch * PER, PER), pl.ds(0, 960), :], out_send.at[batch])

    def out_arrived(batch):
        await_bytes(out.at[pl.ds(batch * PER, PER)], out_recv.at[batch])

    def work(batch):
        row_wait(2 + batch)
        for step in range(PER):
            r = batch * PER + step
            row_item(row_q.at[r], row_k.at[r], row_v.at[r], row_part.at[r], row_level.at[batch], step)
        row_return(batch)
        col_wait(2 + batch)
        col_scores(col_q.at[batch], wide_q, key_by_col, scores, PER)
        col_weights(scores, weights, inverse, col_level.at[batch], batch, PER)
        col_sums(weights, inverse, value_by_col, wide_o, col_part.at[batch], PER)
        col_return(batch)

    def finish(batch):
        return_wait(batch)
        combine(
            home_row_level.at[batch],
            home_row_part,
            home_col_level.at[batch],
            home_col_part,
            home_context,
            batch,
            lax.rem(128 - me * PER, 128),
            PER,
        )
        out_start(batch)

    in_start(0)
    for group in range(2):
        in_next(group)

        @pl.when(active)
        def _(group=group):
            in_wait(group)
            spread(group)
            if group == 0:
                col_wait(0)
                by_column(col_k, wide, key_by_col)

    for batch in range(BATCHES):
        if batch + 1 < BATCHES:
            in_next(2 + batch)

        @pl.when(active)
        def _(batch=batch):
            in_wait(2 + batch)
            spread(2 + batch)
            if batch > 1:
                finish(batch - 2)
            if batch == 1:
                col_wait(1)
                by_column(col_v, wide, value_by_col)
                row_wait(0)
                row_wait(1)
            if batch > 0:
                work(batch - 1)

    @pl.when(active)
    def _():
        work(BATCHES - 1)
        finish(BATCHES - 2)
        finish(BATCHES - 1)
        for group in range(GROUPS):
            spread_sent(group)
        for batch in range(BATCHES):
            return_sent(batch)
            out_sent(batch)

    in_sent(GROUPS - 1)
    for batch in range(BATCHES):
        out_arrived(batch)


def attention(queries, key_vectors, values):
    bf16, f32 = jnp.bfloat16, jnp.float32
    dma = pltpu.SemaphoreType.DMA
    home = pltpu.VMEM((4, 4, 256, 128), bf16)
    rows = pltpu.VMEM((4, 1024, 128), bf16)
    batches = pltpu.VMEM((BATCHES, 4, 4, 2, PER, 32, 128), bf16)
    columns = pltpu.VMEM((4, 4, 2, 4, 32, 128), bf16)
    anywhere = pl.BlockSpec(memory_space=pl.ANY)
    return pl.pallas_call(
        kernel,
        out_shape=jax.ShapeDtypeStruct(queries.shape, bf16),
        in_specs=[anywhere] * 3,
        out_specs=anywhere,
        scratch_shapes=[
            home,
            home,
            home,
            rows,
            rows,
            rows,
            batches,
            columns,
            columns,
            rows,
            pltpu.VMEM((BATCHES, 8 * PER, 1024), f32),
            batches,
            pltpu.VMEM((BATCHES, 32, 128), bf16),
            home,
            pltpu.VMEM((BATCHES, 4, 8 * PER, 256), f32),
            home,
            pltpu.VMEM((BATCHES, 256, 128), bf16),
            home,
            pltpu.VMEM((32, 128, 128), bf16),
            pltpu.VMEM((32, 128, 128), bf16),
            pltpu.VMEM((4096, 128), f32),
            pltpu.VMEM((32 * PER * 32, 128), f32),
            pltpu.VMEM((32 * PER * 32, 128), f32),
            pltpu.VMEM((32, 32 * PER, 128), f32),
            pltpu.VMEM((32, 32 * PER, 128), bf16),
            pltpu.VMEM((32, 32 * PER, 128), f32),
            dma((GROUPS, 8)),
            dma((GROUPS,)),
            dma((GROUPS,)),
            dma((GROUPS,)),
            dma((GROUPS,)),
            dma((GROUPS,)),
            dma((BATCHES, 2)),
            dma((BATCHES, 2)),
            dma((BATCHES, 2)),
            dma((BATCHES, 2)),
            dma((BATCHES,)),
            dma((BATCHES,)),
        ],
        compiler_params=pltpu.CompilerParams(
            collective_id=0, has_side_effects=True, vmem_limit_bytes=60 * 1024 * 1024
        ),
    )(queries, key_vectors, values)


def body(queries, key_vectors, values, out_weight):
    rows_dev, cols_dev, width = queries.shape
    context = attention(queries, key_vectors, values)
    flat = context.reshape(rows_dev * cols_dev, width)
    attended = jnp.dot(flat, out_weight, preferred_element_type=jnp.float32).astype(jnp.bfloat16)
    return attended.reshape(rows_dev, cols_dev, width)


def solution(mesh):
    in_specs = (P("row", "col", None), P("row", "col", None), P("row", "col", None), P())
    out_specs = P("row", "col", None)
    return jax.shard_map(body, mesh=mesh, in_specs=in_specs, out_specs=out_specs, check_vma=False)
```

time: 300 us -> 157 us (0.52)
  Pallas kernels: 0 us -> 154 us
  waiting for transfers between devices: 152 us -> 0 us
  starting transfers between devices: 95.3 us -> 0 us
  local copies, waits for them, and re-layouts: 35.6 us -> 0.01 us
  matrix products: 11 us -> 2.55 us
  other arithmetic: 3.95 us -> 0 us
    pallas_call x0 -> x1, Pallas kernels: none -> 154 us  [attention(): pl.pallas_call(kernel, out_shape=jax.ShapeDtypeStruct(queries.shape, bf16...]
    all_to_all x10 -> x0, waiting for transfers between devices: 152 us -> none  [the longest x2 34.2 us: body(): lax.all_to_all(for_sending(row_parts), 'col', split_axis=1, concat_axis=0...]
    all_to_all x10 -> x0, starting transfers between devices: 95.3 us -> none  [the longest x1 36.9 us: column_attention(): lax.all_to_all(queries, 'row', split_axis=1, concat_axis=0, tiled=True)]
    all_to_all x10 -> x0, local copies, waits for them, and re-layouts: 9.62 us -> none  [the longest x1 1.89 us: row_attention(): lax.all_to_all(sent[1], 'col', split_axis=0, concat_axis=1, tiled=True)]
    dot_general x6 -> x0, matrix products: 9.54 us -> none  [the longest x2 3.69 us: one_item(): jnp.einsum('jd,kd->jk', query_rows, key_rows, preferred_element_type=jnp....]
    unnamed x18 -> x2, local copies, waits for them, and re-layouts: 7.95 us -> 0.01 us
    reshape x4 -> x0, local copies, waits for them, and re-layouts: 6.69 us -> none  [the longest x1 2.17 us: column_attention(): query_cols.reshape(shape_four)]
    convert_element_type x10 -> x0, local copies, waits for them, and re-layouts: 4.42 us -> none  [the longest x2 1.89 us: combine(): second_part.astype(jnp.float32)]
  transfers between devices with their start and end apart: 10 -> 0, of which waited for: 10 -> 0; matrix products, arithmetic and copies ran while one was open for 10% -> 0% of each run, Pallas kernels for 0% -> 0%
where the time goes in v2:
time: 157 us
  Pallas kernels  154 us (98%)
  matrix products  2.55 us (2%)
    pallas_call x1, Pallas kernels, attention(): pl.pallas_call(kernel, out_shape=jax.ShapeDtypeStruct(queries.shape, bf16...  154 us

profile of v2, /device:TPU:1, one launch (start us, length us, event | category | flops | bytes accessed | tf_op | source)
XLA Modules:
  0.0 157.0 jit_solution(5589516799796198626)
XLA Ops:
  0.0 0.0 copy-start
  0.0 154.4 %shard_map.46 = bf16[4,64,1024]{2,1,0:T(8,128)(2,1)} custom-call(bf16[4,64,1024]{2,1,0:T(8,128)(2,1)} %q_in.1, bf16[4,64,1024]{2,1,0:T(8,128)(2,1)} %k_in.1, bf16[4,64,1024]{2,1,0:T(8,128)(2,1)} %v_in.1), custom_call_target="tpu_custom_call" | custom-call | tf_op jit(solution)/shard_map/pallas_call | solution.py:502
  154.4 0.0 copy-done
  154.4 2.5 %convolution_convert_fusion = bf16[256,1024]{1,0:T(8,128)(2,1)} fusion(bf16[256,1024]{1,0:T(8,128)(2,1)} %bitcast.4, bf16[1024,1024]{1,0:T(8,128)(2,1)S(1)} %copy-done), kind=kOutput, calls=%fused_computation | convolution fusion | flops 537133056 | bytes 3145728 | tf_op jit(solution)/shard_map/dot_general | solution.py:557
Async XLA Ops:
  0.0 154.4 %copy-start = (bf16[1024,1024]{1,0:T(8,128)(2,1)S(1)}, bf16[1024,1024]{1,0:T(8,128)(2,1)}, u32[]{:S(2)}) copy-start(bf16[1024,1024]{1,0:T(8,128)(2,1)} %param.7) | copy-start | bytes 6291460

commit v3 on v2

--- a/solution.py
+++ b/solution.py
@@ -13,6 +13,8 @@
 GROUPS = 2 + BATCHES
 BLOCK = 256
 MASKED = -1e30
+RELAYED = 2
+WAY = -4
 MESH = pl.DeviceIdType.MESH
 NT = (((1,), (1,)), ((), ()))
 
@@ -82,7 +84,7 @@
     loop(0, 32, one, 8)
 
 
-def col_weights(scores, weights, inverse, level_ref, batch, per):
+def col_weights(scores, weights, inverse, part_ref, batch, per):
     queries = 32 * per
     at = lax.broadcasted_iota(jnp.int32, (queries, 128), 0)
     lane = lax.broadcasted_iota(jnp.int32, (queries, 128), 1)
@@ -104,7 +106,9 @@
     levels = lax.fori_loop(0, 32, one, jnp.zeros((queries, 128), jnp.float32), unroll=8)
     if queries < 128:
         levels = jnp.concatenate([levels, jnp.zeros((128 - queries, 128), jnp.float32)], axis=0)
-    level_ref[...] = levels.T[:32].astype(jnp.bfloat16)
+    level = levels.T[:32].astype(jnp.bfloat16)
+    for of_me in range(8):
+        part_ref[of_me // 2, 4, of_me % 2, 0] = level
 
 
 def col_sums(weights, inverse, value_by_col, wide, part_ref, per):
@@ -160,11 +164,9 @@
     row_part,
     row_level,
     col_part,
-    col_level,
     home_row_part,
     home_row_level,
     home_col_part,
-    home_col_level,
     home_context,
     key_by_col,
     value_by_col,
@@ -186,6 +188,9 @@
     col_back_recv,
     out_send,
     out_recv,
+    relay,
+    relay_send,
+    relay_recv,
 ):
     at_row, at_col = lax.axis_index("row"), lax.axis_index("col")
     y, z_lo, core = lax.div(at_row, 8), lax.rem(lax.div(at_row, 2), 4), lax.rem(at_row, 2)
@@ -194,6 +199,7 @@
     near = lax.div(z, 2)
     active = lax.rem(z, 2) == 0
     me = y * 2 + core
+    relaying = jnp.logical_and(active, core == 1)
 
     def peer_x(other):
         return device(other, y, z, core)
@@ -250,6 +256,31 @@
         columns = pl.ds(pl.multiple_of(lax.div(source, 4) * 64, 64), 64)
         return of(group, home_k, home_v, home_q).at[lax.rem(source, 4), rows_of(group), columns, :]
 
+    def relay_in(group):
+        src = (k_in, v_in)[group].at[:, :, pl.ds(pl.multiple_of(lax.rem(near + 4, 8) * 128, 128), 128)]
+        return remote(
+            src,
+            relay.at[group],
+            in_send.at[group, lax.rem(near + 4, 8)],
+            relay_recv.at[group],
+            peer_z(lax.rem(z + 16 + WAY, 16)),
+        )
+
+    def relay_on(group):
+        return remote(
+            relay.at[group],
+            in_slot(group, lax.rem(z + 16 - WAY, 16)),
+            relay_send.at[group],
+            in_recv.at[group],
+            peer_z(lax.rem(z + 16 + WAY, 16)),
+        )
+
+    def relay_forward(group):
+        @pl.when(relaying)
+        def _():
+            await_bytes(relay.at[group], relay_recv.at[group])
+            relay_on(group).start()
+
     def in_own(group):
         src = of(group, k_in, v_in, q_in).at[rows_of(group), :, pl.ds(pl.multiple_of(near * 128, 128), 128)]
         return pltpu.make_async_copy(src, in_slot(group, z), in_recv.at[group])
@@ -260,7 +291,19 @@
         def go():
             if before is not None:
                 in_copy(before, head).wait_send()
-            if group is not None:
+            if group is None:
+                return
+            if offset == 4 and group < RELAYED:
+
+                @pl.when(relaying)
+                def _():
+                    relay_in(group).start()
+
+                @pl.when(jnp.logical_not(relaying))
+                def _():
+                    in_copy(group, head).start()
+
+            else:
                 in_copy(group, head).start()
 
         if offset:
@@ -355,18 +398,11 @@
         )
 
     def col_back(batch, other, copy):
-        columns = pl.ds(pl.multiple_of(me * 32, 32), 32)
         copy(
             col_part.at[batch, lax.div(other, 2), :, lax.rem(other, 2)],
-            home_col_part.at[:, pl.ds(batch * PER, PER), columns, :],
-            col_back_send.at[batch, 0],
-            col_back_recv.at[batch, 0],
-        )
-        copy(
-            col_level.at[batch],
-            home_col_level.at[batch, columns, :],
-            col_back_send.at[batch, 1],
-            col_back_recv.at[batch, 1],
+            home_col_part.at[:, pl.ds(batch * PER, PER), pl.ds(pl.multiple_of(me * 32, 32), 32), :],
+            col_back_send.at[batch],
+            col_back_recv.at[batch],
         )
 
     def send_to(device_id):
@@ -387,15 +423,13 @@
         rows = pl.ds(batch * PER, PER)
         await_bytes(home_row_part.at[:, rows], row_back_recv.at[batch, 0])
         await_bytes(home_row_level.at[batch], row_back_recv.at[batch, 1])
-        await_bytes(home_col_part.at[:, rows], col_back_recv.at[batch, 0])
-        await_bytes(home_col_level.at[batch], col_back_recv.at[batch, 1])
+        await_bytes(home_col_part.at[:, rows], col_back_recv.at[batch])
 
     def return_sent(batch):
         rows = pl.ds(batch * PER, PER)
         await_bytes(row_part.at[rows, pl.ds(0, 768), :], row_back_send.at[batch, 0])
         await_bytes(row_level.at[batch, :, pl.ds(0, 768)], row_back_send.at[batch, 1])
-        await_bytes(home_col_part.at[:, rows, pl.ds(0, 224), :], col_back_send.at[batch, 0])
-        await_bytes(home_col_level.at[batch, pl.ds(0, 224), :], col_back_send.at[batch, 1])
+        await_bytes(home_col_part.at[:, rows, pl.ds(0, 224), :], col_back_send.at[batch])
 
     def out_slot(batch, head):
         return out.at[pl.ds(batch * PER, PER), :, pl.ds(pl.multiple_of(head * 128, 128), 128)]
@@ -419,15 +453,17 @@
     def out_arrived(batch):
         await_bytes(out.at[pl.ds(batch * PER, PER)], out_recv.at[batch])
 
-    def work(batch):
+    def row_work(batch):
         row_wait(2 + batch)
         for step in range(PER):
             r = batch * PER + step
             row_item(row_q.at[r], row_k.at[r], row_v.at[r], row_part.at[r], row_level.at[batch], step)
         row_return(batch)
+
+    def col_work(batch):
         col_wait(2 + batch)
         col_scores(col_q.at[batch], wide_q, key_by_col, scores, PER)
-        col_weights(scores, weights, inverse, col_level.at[batch], batch, PER)
+        col_weights(scores, weights, inverse, col_part.at[batch], batch, PER)
         col_sums(weights, inverse, value_by_col, wide_o, col_part.at[batch], PER)
         col_return(batch)
 
@@ -436,7 +472,7 @@
         combine(
             home_row_level.at[batch],
             home_row_part,
-            home_col_level.at[batch],
+            home_col_part.at[4, batch * PER],
             home_col_part,
             home_context,
             batch,
@@ -451,6 +487,7 @@
 
         @pl.when(active)
         def _(group=group):
+            relay_forward(group)
             in_wait(group)
             spread(group)
             if group == 0:
@@ -465,23 +502,32 @@
         def _(batch=batch):
             in_wait(2 + batch)
             spread(2 + batch)
-            if batch > 1:
-                finish(batch - 2)
+            if batch == 3:
+                finish(0)
             if batch == 1:
                 col_wait(1)
                 by_column(col_v, wide, value_by_col)
                 row_wait(0)
                 row_wait(1)
             if batch > 0:
-                work(batch - 1)
+                row_work(batch - 1)
+                col_work(batch - 1)
 
     @pl.when(active)
     def _():
-        work(BATCHES - 1)
+        finish(1)
+        row_work(BATCHES - 1)
+        col_work(BATCHES - 1)
         finish(BATCHES - 2)
         finish(BATCHES - 1)
         for group in range(GROUPS):
             spread_sent(group)
+
+        @pl.when(relaying)
+        def _():
+            for group in range(RELAYED):
+                await_bytes(relay.at[group], relay_send.at[group])
+
         for batch in range(BATCHES):
             return_sent(batch)
             out_sent(batch)
@@ -496,7 +542,6 @@
     dma = pltpu.SemaphoreType.DMA
     home = pltpu.VMEM((4, 4, 256, 128), bf16)
     rows = pltpu.VMEM((4, 1024, 128), bf16)
-    batches = pltpu.VMEM((BATCHES, 4, 4, 2, PER, 32, 128), bf16)
     columns = pltpu.VMEM((4, 4, 2, 4, 32, 128), bf16)
     anywhere = pl.BlockSpec(memory_space=pl.ANY)
     return pl.pallas_call(
@@ -511,17 +556,15 @@
             rows,
             rows,
             rows,
-            batches,
+            pltpu.VMEM((BATCHES, 4, 4, 2, PER, 32, 128), bf16),
             columns,
             columns,
             rows,
             pltpu.VMEM((BATCHES, 8 * PER, 1024), f32),
-            batches,
-            pltpu.VMEM((BATCHES, 32, 128), bf16),
+            pltpu.VMEM((BATCHES, 4, 5, 2, PER, 32, 128), bf16),
             home,
             pltpu.VMEM((BATCHES, 4, 8 * PER, 256), f32),
-            home,
-            pltpu.VMEM((BATCHES, 256, 128), bf16),
+            pltpu.VMEM((5, 4, 256, 128), bf16),
             home,
             pltpu.VMEM((32, 128, 128), bf16),
             pltpu.VMEM((32, 128, 128), bf16),
@@ -539,10 +582,13 @@
             dma((GROUPS,)),
             dma((BATCHES, 2)),
             dma((BATCHES, 2)),
-            dma((BATCHES, 2)),
-            dma((BATCHES, 2)),
             dma((BATCHES,)),
             dma((BATCHES,)),
+            dma((BATCHES,)),
+            dma((BATCHES,)),
+            pltpu.VMEM((RELAYED, 4, 64, 128), bf16),
+            dma((RELAYED,)),
+            dma((RELAYED,)),
         ],
         compiler_params=pltpu.CompilerParams(
             collective_id=0, has_side_effects=True, vmem_limit_bytes=60 * 1024 * 1024

time: 157 us -> 143 us (0.911)
  Pallas kernels: 154 us -> 139 us
    pallas_call x1, Pallas kernels: 154 us -> 139 us  [attention(): pl.pallas_call(kernel, out_shape=jax.ShapeDtypeStruct(queries.shape, bf16...]
where the time goes in v3:
time: 143 us; the launch traced here: 142 us
  Pallas kernels  139 us (97%)
  matrix products  2.55 us (2%)
    pallas_call x1, Pallas kernels, attention(): pl.pallas_call(kernel, out_shape=jax.ShapeDtypeStruct(queries.shape, bf16...  139 us

profile of v3, /device:TPU:1, one launch (start us, length us, event | category | flops | bytes accessed | tf_op | source)
XLA Modules:
  0.0 141.9 jit_solution(14299587298122972848)
XLA Ops:
  0.0 0.0 copy-start
  0.0 139.4 %shard_map.46 = bf16[4,64,1024]{2,1,0:T(8,128)(2,1)} custom-call(bf16[4,64,1024]{2,1,0:T(8,128)(2,1)} %q_in.1, bf16[4,64,1024]{2,1,0:T(8,128)(2,1)} %k_in.1, bf16[4,64,1024]{2,1,0:T(8,128)(2,1)} %v_in.1), custom_call_target="tpu_custom_call" | custom-call | tf_op jit(solution)/shard_map/pallas_call | solution.py:547
  139.4 0.0 copy-done
  139.4 2.5 %convolution_convert_fusion = bf16[256,1024]{1,0:T(8,128)(2,1)} fusion(bf16[256,1024]{1,0:T(8,128)(2,1)} %bitcast.4, bf16[1024,1024]{1,0:T(8,128)(2,1)S(1)} %copy-done), kind=kOutput, calls=%fused_computation | convolution fusion | flops 537133056 | bytes 3145728 | tf_op jit(solution)/shard_map/dot_general | solution.py:603
Async XLA Ops:
  0.0 139.4 %copy-start = (bf16[1024,1024]{1,0:T(8,128)(2,1)S(1)}, bf16[1024,1024]{1,0:T(8,128)(2,1)}, u32[]{:S(2)}) copy-start(bf16[1024,1024]{1,0:T(8,128)(2,1)} %param.7) | copy-start | bytes 6291460

commit v4 on v3

--- a/solution.py
+++ b/solution.py
@@ -51,7 +51,7 @@
     def one(c):
         target[c] = wide[pl.ds(c, 128, stride=32), :].astype(jnp.bfloat16)
 
-    loop(0, 32, one, 8)
+    loop(0, 32, one, 16)
 
 
 def row_item(query_ref, key_ref, value_ref, part_ref, level_ref, step):
@@ -81,7 +81,7 @@
         query = wide[pl.ds(c, 32 * per, stride=32), :].astype(jnp.bfloat16)
         scores[c] = lax.dot_general(query, key_by_col[c], NT, preferred_element_type=jnp.float32)
 
-    loop(0, 32, one, 8)
+    loop(0, 32, one, 16)
 
 
 def col_weights(scores, weights, inverse, part_ref, batch, per):
@@ -103,7 +103,7 @@
         inverse[c] = jnp.broadcast_to(1.0 / total, (queries, 128))
         return jnp.where(lane == c, best * SCALE + jnp.log(total), levels)
 
-    levels = lax.fori_loop(0, 32, one, jnp.zeros((queries, 128), jnp.float32), unroll=8)
+    levels = lax.fori_loop(0, 32, one, jnp.zeros((queries, 128), jnp.float32), unroll=16)
     if queries < 128:
         levels = jnp.concatenate([levels, jnp.zeros((128 - queries, 128), jnp.float32)], axis=0)
     level = levels.T[:32].astype(jnp.bfloat16)
@@ -116,7 +116,7 @@
         summed = jnp.dot(weights[c], value_by_col[c], preferred_element_type=jnp.float32)
         wide[pl.ds(c, 32 * per, stride=32), :] = summed * inverse[c]
 
-    loop(0, 32, one, 8)
+    loop(0, 32, one, 16)
 
     def narrow(block):
         of_z, of_me = lax.div(block, 8), lax.rem(block, 8)

time: 143 us -> 142 us (level)
  no operation moved by 1% of the time
where the time goes in v4:
time: 142 us
  Pallas kernels  139 us (98%)
  matrix products  2.55 us (2%)
    pallas_call x1, Pallas kernels, attention(): pl.pallas_call(kernel, out_shape=jax.ShapeDtypeStruct(queries.shape, bf16...  139 us

profile of v4, /device:TPU:1, one launch (start us, length us, event | category | flops | bytes accessed | tf_op | source)
XLA Modules:
  0.0 141.8 jit_solution(3316978445344474979)
XLA Ops:
  0.0 0.0 copy-start
  0.0 139.2 %shard_map.46 = bf16[4,64,1024]{2,1,0:T(8,128)(2,1)} custom-call(bf16[4,64,1024]{2,1,0:T(8,128)(2,1)} %q_in.1, bf16[4,64,1024]{2,1,0:T(8,128)(2,1)} %k_in.1, bf16[4,64,1024]{2,1,0:T(8,128)(2,1)} %v_in.1), custom_call_target="tpu_custom_call" | custom-call | tf_op jit(solution)/shard_map/pallas_call | solution.py:547
  139.2 0.0 copy-done
  139.2 2.5 %convolution_convert_fusion = bf16[256,1024]{1,0:T(8,128)(2,1)} fusion(bf16[256,1024]{1,0:T(8,128)(2,1)} %bitcast.4, bf16[1024,1024]{1,0:T(8,128)(2,1)S(1)} %copy-done), kind=kOutput, calls=%fused_computation | convolution fusion | flops 537133056 | bytes 3145728 | tf_op jit(solution)/shard_map/dot_general | solution.py:603
Async XLA Ops:
  0.0 139.2 %copy-start = (bf16[1024,1024]{1,0:T(8,128)(2,1)S(1)}, bf16[1024,1024]{1,0:T(8,128)(2,1)}, u32[]{:S(2)}) copy-start(bf16[1024,1024]{1,0:T(8,128)(2,1)} %param.7) | copy-start | bytes 6291460
